TPU v7x, 32 devices: a whole 2x2x4 slice. The times are simulated.
32 devices in a mesh: row: 2 (over core), col: 16 (over z, y, x).
Axes of the slice: x: 2, y: 2, z: 4, core: 2. Of those that a mesh axis runs over, the one named last changes fastest.
Arguments:
- tokens: bfloat16 [2, 16384, 512], P(None, 'col', 'row'), may hold values from -8 to 8
- memory: bfloat16 [2, 16384, 512], P(None, 'col', 'row'), may hold values from -6 to 6
- cotangent: bfloat16 [2, 16384, 512], P(None, 'col', 'row'), may hold values from -6 to 6
- segments: int32 [2, 16384], P(None, 'col'), may hold values from 0 to 1023, as said below
- padding: int32 [2, 16384], P(None, 'col'), may hold values from 0 to 1, as said below
- self_query: bfloat16 [512, 512], P('row', 'col'), may hold values from -0.25 to 0.25
- self_key: bfloat16 [512, 512], P('row', 'col'), may hold values from -0.25 to 0.25
- self_value: bfloat16 [512, 512], P('row', 'col'), may hold values from -0.25 to 0.25
- self_output: bfloat16 [512, 512], P('row', 'col'), may hold values from -0.75 to 0.75
- cross_query: bfloat16 [512, 512], P('row', 'col'), may hold values from -0.25 to 0.25
- cross_key: bfloat16 [512, 512], P('row', 'col'), may hold values from -0.25 to 0.25
- cross_value: bfloat16 [512, 512], P('row', 'col'), may hold values from -0.25 to 0.25
- cross_output: bfloat16 [512, 512], P('row', 'col'), may hold values from -3 to 3
- feed_up: bfloat16 [512, 2048], P('row', 'col'), may hold values from -0.25 to 0.25
- feed_down: bfloat16 [2048, 512], P('row', 'col'), may hold values from -0.125 to 0.125
- norm_gain: float32 [3, 512], P(None, 'row'), may hold values from 0.5 to 1.5
- norm_bias: float32 [3, 512], P(None, 'row'), may hold values from -3 to 3
- omegas: float32 [3, 512], P(None, 'row'), may hold values from 0.5 to 1.5
Outputs:
- layer_out: bfloat16 [2, 16384, 512], P(None, 'col', 'row')
- tokens_grad: float32 [2, 16384, 512], P(None, 'col', 'row')
- memory_grad: float32 [2, 16384, 512], P(None, 'col', 'row')
- self_query_grad: float32 [512, 512], P('row', 'col')
- self_key_grad: float32 [512, 512], P('row', 'col')
- self_value_grad: float32 [512, 512], P('row', 'col')
- self_output_grad: float32 [512, 512], P('row', 'col')
- cross_query_grad: float32 [512, 512], P('row', 'col')
- cross_key_grad: float32 [512, 512], P('row', 'col')
- cross_value_grad: float32 [512, 512], P('row', 'col')
- cross_output_grad: float32 [512, 512], P('row', 'col')
- feed_up_grad: float32 [512, 2048], P('row', 'col')
- feed_down_grad: float32 [2048, 512], P('row', 'col')
- norm_gain_grad: float32 [3, 512], P(None, ('row', 'col'))
- norm_bias_grad: float32 [3, 512], P(None, ('row', 'col'))
- omegas_gradient: float32 [3, 512], P(None, ('row', 'col'))
Inputs may be any that keep to these rules, and one draw needn't show every extreme that they name: `segments`: in each sequence of 1024 tokens, a token's number is the position within the sequence of the first token of its document; numbers never fall along a sequence, and the sequence's last token begins a document of its own. `padding`: in each sequence the ones come first and the zeros last; each sequence ends in 1 to 256 zeros.
All inputs are finite; a program needn't handle non-finite values.
Results may differ from a plain program's by a relative error of at most 0.04.
Values may be sent and summed in bfloat16 or wider, within the bound.
A program may use at most 192 MiB of HBM per device.

v0:
```python
import jax
import jax.numpy as jnp
from jax import lax
from jax.sharding import PartitionSpec as P

HD = 64


EPSILON = 1e-05
MASKED = -1e30


def row_total(acts_in, matrices):
    partial_value = jnp.einsum("nd,sdo->sno", acts_in, matrices, preferred_element_type=jnp.float32)
    return lax.psum_scatter(partial_value, "row", scatter_dimension=2, tiled=True)


def widen(gradient):
    return lax.all_gather(gradient, "row", axis=2, tiled=True)


def smooth_gate(values):
    return jax.nn.gelu(values, approximate=True)


def layer_norm(resid, gain_row, bias_row):
    features = resid.shape[1] * lax.axis_size("row")
    average = lax.psum(jnp.sum(resid, axis=1), "row") / features
    centred = resid - average[:, None]
    variance = lax.psum(jnp.sum(centred * centred, axis=1), "row") / features
    factor = lax.rsqrt(variance + EPSILON)
    normed = (resid - average[:, None]) * factor[:, None]
    return (normed * gain_row + bias_row, normed, factor)


def norm_back(upstream, normed, factor, gain_row):
    features = normed.shape[1] * lax.axis_size("row")
    scaled = upstream * gain_row
    first_sum, second_sum = lax.psum(
        (jnp.sum(scaled, axis=1), jnp.sum(scaled * normed, axis=1)), "row"
    )
    before = factor[:, None] * (
        scaled - first_sum[:, None] / features - normed * (second_sum[:, None] / features)
    )
    return (before, jnp.sum(upstream * normed, axis=0), jnp.sum(upstream, axis=0))


def self_mask(segment_row, padding_row):
    length = segment_row.shape[0]
    columns = jnp.arange(length, dtype=jnp.int32)

    def allowed(offset, block_rows):
        rows_here = offset + jnp.arange(block_rows, dtype=jnp.int32)
        segment_here = lax.dynamic_slice_in_dim(segment_row, offset, block_rows, 0)
        same_doc = segment_here[:, None] == segment_row[None, :]
        causal = columns[None, :] <= rows_here[:, None]
        live_key = padding_row[None, :] == 1
        return same_doc & causal & live_key | (columns[None, :] == rows_here[:, None])

    return allowed


def block_scores(query_block, keys_in, allowed, offset, block_rows, factor):
    scores = (
        jnp.einsum("qhe,khe->hqk", query_block, keys_in, preferred_element_type=jnp.float32)
        * factor
    )
    if allowed is not None:
        scores = jnp.where(allowed(offset, block_rows)[None], scores, MASKED)
    return scores


def attend(query_rows, keys_in, values_in, allowed):
    length, heads_here, head_size = query_rows.shape
    block_rows = min(512, length)
    blocks = length // block_rows
    factor = head_size ** (-0.5)

    def one_block(position):
        offset = position * block_rows
        query_block = lax.dynamic_slice_in_dim(query_rows, offset, block_rows, 0)
        scores = block_scores(query_block, keys_in, allowed, offset, block_rows, factor)
        highest = jnp.max(scores, axis=2, keepdims=True)
        raised = jnp.exp(scores - highest)
        totals = jnp.sum(raised, axis=2, keepdims=True)
        weighting = (raised / totals).astype(jnp.bfloat16)
        context = jnp.einsum(
            "hqk,khe->qhe", weighting, values_in, preferred_element_type=jnp.float32
        )
        return (context, (highest + jnp.log(totals))[:, :, 0])

    context, logsum = lax.map(one_block, jnp.arange(blocks, dtype=jnp.int32))
    return (context.reshape(length, heads_here, head_size), logsum)


def attend_back(query_rows, keys_in, values_in, logsum, upstream, allowed):
    length, heads_here, head_size = query_rows.shape
    block_rows = min(512, length)
    blocks = length // block_rows
    factor = head_size ** (-0.5)

    def one_block(carry, position):
        key_grad, value_grad = carry
        offset = position * block_rows
        query_block = lax.dynamic_slice_in_dim(query_rows, offset, block_rows, 0)
        upstream_block = lax.dynamic_slice_in_dim(upstream, offset, block_rows, 0)
        scores = block_scores(query_block, keys_in, allowed, offset, block_rows, factor)
        block_logsum = lax.dynamic_index_in_dim(logsum, position, 0, keepdims=False)
        weighting = jnp.exp(scores - block_logsum[:, :, None])
        prob_grad = jnp.einsum(
            "qhe,khe->hqk", upstream_block, values_in, preferred_element_type=jnp.float32
        )
        value_grad = value_grad + jnp.einsum(
            "hqk,qhe->khe",
            weighting.astype(jnp.bfloat16),
            upstream_block,
            preferred_element_type=jnp.float32,
        )
        inner_sum = jnp.sum(prob_grad * weighting, axis=2, keepdims=True)
        score_grad = (weighting * (prob_grad - inner_sum)).astype(jnp.bfloat16)
        query_grad = (
            jnp.einsum("hqk,khe->qhe", score_grad, keys_in, preferred_element_type=jnp.float32)
            * factor
        )
        key_grad = (
            key_grad
            + jnp.einsum(
                "hqk,qhe->khe", score_grad, query_block, preferred_element_type=jnp.float32
            )
            * factor
        )
        return ((key_grad, value_grad), query_grad)

    zeros = jnp.zeros(keys_in.shape, jnp.float32)
    (key_grad, value_grad), query_grad = lax.scan(
        one_block, (zeros, zeros), jnp.arange(blocks, dtype=jnp.int32)
    )
    return (query_grad.reshape(length, heads_here, head_size), key_grad, value_grad)


def body(
    tokens,
    memory,
    cotangent,
    segments,
    padding,
    self_query,
    self_key,
    self_value,
    self_output,
    cross_query,
    cross_key,
    cross_value,
    cross_output,
    feed_up,
    feed_down,
    norm_gain,
    norm_bias,
    omegas,
):
    weights_all = (
        lax.all_gather(self_query, "col", axis=1, tiled=True),
        lax.all_gather(self_key, "col", axis=1, tiled=True),
        lax.all_gather(self_value, "col", axis=1, tiled=True),
        lax.all_gather(self_output, "col", axis=1, tiled=True),
        lax.all_gather(cross_query, "col", axis=1, tiled=True),
        lax.all_gather(cross_key, "col", axis=1, tiled=True),
        lax.all_gather(cross_value, "col", axis=1, tiled=True),
        lax.all_gather(cross_output, "col", axis=1, tiled=True),
        lax.all_gather(feed_up, "col", axis=1, tiled=True),
        lax.all_gather(feed_down, "col", axis=1, tiled=True),
    )
    self_weight_bundle = jnp.stack([weights_all[0], weights_all[1], weights_all[2]])
    cross_weight_bundle = jnp.stack([weights_all[5], weights_all[6]])
    half_width = tokens.shape[2]

    def micro_step(totals, inputs):
        tokens_microbatch, memory_microbatch, cotangent_mb, segment_mb, padding_mb = inputs
        length = tokens_microbatch.shape[0]
        memory_rows = memory_microbatch.shape[0]
        heads_here = half_width // HD
        input_float = tokens_microbatch.astype(jnp.float32)
        projected = row_total(tokens_microbatch, self_weight_bundle).astype(jnp.bfloat16)
        query_rows = projected[0].reshape(length, heads_here, HD)
        keys_self = projected[1].reshape(length, heads_here, HD)
        values_self = projected[2].reshape(length, heads_here, HD)
        allowed = self_mask(segment_mb, padding_mb)
        context, self_logsum = attend(query_rows, keys_self, values_self, allowed)
        context_low = context.astype(jnp.bfloat16).reshape(length, half_width)
        attn_out = row_total(context_low, weights_all[3][None])[0]
        first_norm, first_normed, first_factor = layer_norm(
            omegas[0] * input_float + attn_out, norm_gain[0], norm_bias[0]
        )
        first_low = first_norm.astype(jnp.bfloat16)
        probes = row_total(first_low, weights_all[4][None])[0].astype(jnp.bfloat16)
        memory_proj = row_total(memory_microbatch, cross_weight_bundle).astype(jnp.bfloat16)
        probes = probes.reshape(length, heads_here, HD)
        anchors = memory_proj[0].reshape(memory_rows, heads_here, HD)
        payload = memory_proj[1].reshape(memory_rows, heads_here, HD)
        cross_context, cross_logsum = attend(probes, anchors, payload, None)
        cross_low = cross_context.astype(jnp.bfloat16).reshape(length, half_width)
        cross_result = row_total(cross_low, weights_all[7][None])[0]
        second_norm, second_normed, second_factor = layer_norm(
            omegas[1] * first_norm + cross_result, norm_gain[1], norm_bias[1]
        )
        second_low = second_norm.astype(jnp.bfloat16)
        hidden_pre = row_total(second_low, weights_all[8][None])[0]
        hidden_value, gate_pullback = jax.vjp(smooth_gate, hidden_pre)
        hidden_low = hidden_value.astype(jnp.bfloat16)
        feed_result = row_total(hidden_low, weights_all[9][None])[0]
        output_norm, output_normed, output_factor = layer_norm(
            omegas[2] * second_norm + feed_result, norm_gain[2], norm_bias[2]
        )
        upstream = cotangent_mb.astype(jnp.float32)
        third_grad, gain_three, bias_three = norm_back(
            upstream, output_normed, output_factor, norm_gain[2]
        )
        omega_three = jnp.sum(third_grad * second_norm, axis=0)
        second_grad = omegas[2] * third_grad
        feed_grad = widen(third_grad.astype(jnp.bfloat16)[None])[0]
        narrowing_grad = jnp.einsum(
            "nf,nd->fd", hidden_low, feed_grad, preferred_element_type=jnp.float32
        )
        hidden_grad = jnp.einsum(
            "nd,fd->nf", feed_grad, weights_all[9], preferred_element_type=jnp.float32
        )
        gated_grad_low = gate_pullback(hidden_grad)[0].astype(jnp.bfloat16)
        gated_full = widen(gated_grad_low[None])[0]
        widening_grad = jnp.einsum(
            "nd,nf->df", second_low, gated_full, preferred_element_type=jnp.float32
        )
        second_grad = second_grad + jnp.einsum(
            "nf,df->nd", gated_full, weights_all[8], preferred_element_type=jnp.float32
        )
        middle_grad, gain_two, bias_two = norm_back(
            second_grad, second_normed, second_factor, norm_gain[1]
        )
        omega_two = jnp.sum(middle_grad * first_norm, axis=0)
        first_grad = omegas[1] * middle_grad
        cross_up = widen(middle_grad.astype(jnp.bfloat16)[None])[0]
        closing_grad = jnp.einsum(
            "nd,ne->de", cross_low, cross_up, preferred_element_type=jnp.float32
        )
        cross_ctx_grad = jnp.einsum(
            "ne,de->nd", cross_up, weights_all[7], preferred_element_type=jnp.float32
        )
        cross_ctx_grad = cross_ctx_grad.astype(jnp.bfloat16).reshape(length, heads_here, HD)
        probes_grad, anchors_grad, payload_grad = attend_back(
            probes, anchors, payload, cross_logsum, cross_ctx_grad, None
        )
        probes_full = widen(probes_grad.reshape(length, half_width).astype(jnp.bfloat16)[None])[0]
        probing_grad = jnp.einsum(
            "nd,ne->de", first_low, probes_full, preferred_element_type=jnp.float32
        )
        first_grad = first_grad + jnp.einsum(
            "ne,de->nd", probes_full, weights_all[4], preferred_element_type=jnp.float32
        )
        memory_entire = widen(
            jnp.stack(
                [
                    anchors_grad.reshape(memory_rows, half_width),
                    payload_grad.reshape(memory_rows, half_width),
                ]
            ).astype(jnp.bfloat16)
        )
        reading_grad = jnp.einsum(
            "il,ciw->clw", memory_microbatch, memory_entire, preferred_element_type=jnp.float32
        )
        memory_grad = jnp.einsum(
            "faq,fkq->ak", memory_entire, cross_weight_bundle, preferred_element_type=jnp.float32
        )
        inner_grad, gain_one, bias_one = norm_back(
            first_grad, first_normed, first_factor, norm_gain[0]
        )
        omega_one = jnp.sum(inner_grad * input_float, axis=0)
        input_grad = omegas[0] * inner_grad
        self_up = widen(inner_grad.astype(jnp.bfloat16)[None])[0]
        leaving_grad = jnp.einsum(
            "nd,ne->de", context_low, self_up, preferred_element_type=jnp.float32
        )
        context_grad = jnp.einsum(
            "ne,de->nd", self_up, weights_all[3], preferred_element_type=jnp.float32
        )
        context_grad = context_grad.astype(jnp.bfloat16).reshape(length, heads_here, HD)
        query_grad, key_grad, value_grad = attend_back(
            query_rows, keys_self, values_self, self_logsum, context_grad, allowed
        )
        self_entire = widen(
            jnp.stack(
                [
                    query_grad.reshape(length, half_width),
                    key_grad.reshape(length, half_width),
                    value_grad.reshape(length, half_width),
                ]
            ).astype(jnp.bfloat16)
        )
        entry_grad = jnp.einsum(
            "il,ciw->clw", tokens_microbatch, self_entire, preferred_element_type=jnp.float32
        )
        input_grad = input_grad + jnp.einsum(
            "faq,fkq->ak", self_entire, self_weight_bundle, preferred_element_type=jnp.float32
        )
        grads = (
            entry_grad[0],
            entry_grad[1],
            entry_grad[2],
            leaving_grad,
            probing_grad,
            reading_grad[0],
            reading_grad[1],
            closing_grad,
            widening_grad,
            narrowing_grad,
            jnp.stack([gain_one, gain_two, gain_three]),
            jnp.stack([bias_one, bias_two, bias_three]),
            jnp.stack([omega_one, omega_two, omega_three]),
        )
        totals = tuple((summed + added for summed, added in zip(totals, grads)))
        return (totals, (output_norm.astype(jnp.bfloat16), input_grad, memory_grad))

    shapes = (
        weights_all[0].shape,
        weights_all[1].shape,
        weights_all[2].shape,
        weights_all[3].shape,
        weights_all[4].shape,
        weights_all[5].shape,
        weights_all[6].shape,
        weights_all[7].shape,
        weights_all[8].shape,
        weights_all[9].shape,
        (3, half_width),
        (3, half_width),
        (3, half_width),
    )
    zeros = tuple((jnp.zeros(shape_one, jnp.float32) for shape_one in shapes))
    totals, (outputs, input_grads, memory_grads) = lax.scan(
        micro_step, zeros, (tokens, memory, cotangent, segments, padding)
    )
    finals = (
        lax.psum_scatter(totals[0], "col", scatter_dimension=1, tiled=True),
        lax.psum_scatter(totals[1], "col", scatter_dimension=1, tiled=True),
        lax.psum_scatter(totals[2], "col", scatter_dimension=1, tiled=True),
        lax.psum_scatter(totals[3], "col", scatter_dimension=1, tiled=True),
        lax.psum_scatter(totals[4], "col", scatter_dimension=1, tiled=True),
        lax.psum_scatter(totals[5], "col", scatter_dimension=1, tiled=True),
        lax.psum_scatter(totals[6], "col", scatter_dimension=1, tiled=True),
        lax.psum_scatter(totals[7], "col", scatter_dimension=1, tiled=True),
        lax.psum_scatter(totals[8], "col", scatter_dimension=1, tiled=True),
        lax.psum_scatter(totals[9], "col", scatter_dimension=1, tiled=True),
        lax.psum_scatter(totals[10], "col", scatter_dimension=1, tiled=True),
        lax.psum_scatter(totals[11], "col", scatter_dimension=1, tiled=True),
        lax.psum_scatter(totals[12], "col", scatter_dimension=1, tiled=True),
    )
    return (
        outputs,
        input_grads,
        memory_grads,
        finals[0],
        finals[1],
        finals[2],
        finals[3],
        finals[4],
        finals[5],
        finals[6],
        finals[7],
        finals[8],
        finals[9],
        finals[10],
        finals[11],
        finals[12],
    )


def solution(mesh):
    return jax.shard_map(
        body,
        mesh=mesh,
        in_specs=(
            P(None, "col", "row"),
            P(None, "col", "row"),
            P(None, "col", "row"),
            P(None, "col"),
            P(None, "col"),
            P("row", "col"),
            P("row", "col"),
            P("row", "col"),
            P("row", "col"),
            P("row", "col"),
            P("row", "col"),
            P("row", "col"),
            P("row", "col"),
            P("row", "col"),
            P("row", "col"),
            P(None, "row"),
            P(None, "row"),
            P(None, "row"),
        ),
        out_specs=(
            P(None, "col", "row"),
            P(None, "col", "row"),
            P(None, "col", "row"),
            P("row", "col"),
            P("row", "col"),
            P("row", "col"),
            P("row", "col"),
            P("row", "col"),
            P("row", "col"),
            P("row", "col"),
            P("row", "col"),
            P("row", "col"),
            P("row", "col"),
            P(None, ("row", "col")),
            P(None, ("row", "col")),
            P(None, ("row", "col")),
        ),
        check_vma=False,
    )
```

profile of v0, /device:TPU:0, one launch (start us, length us, event | category | flops | bytes accessed | tf_op | source)
XLA Modules:
  0.0 2069.5 jit_solution(10476661565591205646)
XLA Ops:
  8.9 44.2 %all_gather.72 = bf16[256,512]{0,1:T(8,128)(2,1)S(1)} all-gather(bf16[256,32]{0,1:T(8,128)(2,1)} %param.33), channel_id=1, replica_groups=mesh['row'=2,'col'=16] {'col'}, dimensions={1}, use_global_device_ids=true | all-gather | bytes 278528 | tf_op jit(solution)/shard_map/all_gather | solution.py:162
  53.1 37.6 %all_gather.73 = bf16[256,512]{0,1:T(8,128)(2,1)S(1)} all-gather(bf16[256,32]{0,1:T(8,128)(2,1)} %param.34), channel_id=1, replica_groups=mesh['row'=2,'col'=16] {'col'}, dimensions={1}, use_global_device_ids=true | all-gather | bytes 278528 | tf_op jit(solution)/shard_map/all_gather | solution.py:163
  90.7 39.8 %all_gather.74 = bf16[256,512]{0,1:T(8,128)(2,1)S(1)} all-gather(bf16[256,32]{0,1:T(8,128)(2,1)} %param.35), channel_id=1, replica_groups=mesh['row'=2,'col'=16] {'col'}, dimensions={1}, use_global_device_ids=true | all-gather | bytes 278528 | tf_op jit(solution)/shard_map/all_gather | solution.py:164
  131.7 37.4 %all_gather.75 = bf16[256,512]{0,1:T(8,128)(2,1)S(1)} all-gather(bf16[256,32]{0,1:T(8,128)(2,1)} %param.36), channel_id=1, replica_groups=mesh['row'=2,'col'=16] {'col'}, dimensions={1}, use_global_device_ids=true | all-gather | bytes 278528 | tf_op jit(solution)/shard_map/all_gather | solution.py:165
  169.3 38.9 %all_gather.76 = bf16[256,512]{0,1:T(8,128)(2,1)S(1)} all-gather(bf16[256,32]{0,1:T(8,128)(2,1)S(1)} %copy-done.80), channel_id=1, replica_groups=mesh['row'=2,'col'=16] {'col'}, dimensions={1}, use_global_device_ids=true | all-gather | bytes 278528 | tf_op jit(solution)/shard_map/all_gather | solution.py:166
  209.1 36.9 %all_gather.77 = bf16[256,512]{0,1:T(8,128)(2,1)S(1)} all-gather(bf16[256,32]{0,1:T(8,128)(2,1)S(1)} %copy-done.81), channel_id=1, replica_groups=mesh['row'=2,'col'=16] {'col'}, dimensions={1}, use_global_device_ids=true | all-gather | bytes 278528 | tf_op jit(solution)/shard_map/all_gather | solution.py:167
  246.0 38.9 %all_gather.78 = bf16[256,512]{0,1:T(8,128)(2,1)S(1)} all-gather(bf16[256,32]{0,1:T(8,128)(2,1)S(1)} %copy-done.82), channel_id=1, replica_groups=mesh['row'=2,'col'=16] {'col'}, dimensions={1}, use_global_device_ids=true | all-gather | bytes 278528 | tf_op jit(solution)/shard_map/all_gather | solution.py:168
  285.9 36.8 %all_gather.79 = bf16[256,512]{0,1:T(8,128)(2,1)S(1)} all-gather(bf16[256,32]{0,1:T(8,128)(2,1)S(1)} %copy-done.83), channel_id=1, replica_groups=mesh['row'=2,'col'=16] {'col'}, dimensions={1}, use_global_device_ids=true | all-gather | bytes 278528 | tf_op jit(solution)/shard_map/all_gather | solution.py:169
  325.9 741.2 %while.162 = (s32[]{:T(128)}, f32[256,512]{0,1:T(8,128)}, f32[256,512]{0,1:T(8,128)}, f32[256,512]{0,1:T(8,128)}, f32[256,512]{1,0:T(8,128)}, /*index=5*/f32[256...) while((s32[]{:T(128)}, f32[256,512]{0,1:T(8,128)}, ...), condition=%wide.region_55.56_spmd.clone, body=%wide.region_0.55_spmd.clone.sunk | while | flops 16840147968 | bytes 804348224 | solution.py:337
  628.9 32.8 %while.166 = (s32[]{:T(128)}, f32[1024,4,64]{0,2,1:T(8,128)S(1)}, f32[1024,4,64]{0,2,1:T(8,128)}, bf16[2,512,4,64]{1,3,2,0:T(8,128)(2,1)}, s32[2]{0:T(128)S(1)},...) while((s32[]{:T(128)}, f32[1024,4,64]{0,2,1:T(8,128)S(1)}, ...), condition=%wide.region_45.45_spmd.clone.clone, body=%wide.region_43.44_spmd.clone.clone.sunk | while | flops 1378221568 | bytes 87110072 | solution.py:135
  999.3 32.8 %while.166 = (s32[]{:T(128)}, f32[1024,4,64]{0,2,1:T(8,128)S(1)}, f32[1024,4,64]{0,2,1:T(8,128)}, bf16[2,512,4,64]{1,3,2,0:T(8,128)(2,1)}, s32[2]{0:T(128)S(1)},...) while((s32[]{:T(128)}, f32[1024,4,64]{0,2,1:T(8,128)S(1)}, ...), condition=%wide.region_45.45_spmd.clone.clone, body=%wide.region_43.44_spmd.clone.clone.sunk | while | flops 1378221568 | bytes 87110072 | solution.py:135
  1083.4 63.9 %reduce-scatter.47.cloned.1.call-done = f32[16,3]{1,0:T(8,128)} async-done(((f32[256,3]{1,0:T(8,128)}), f32[16,3]{1,0:T(8,128)}) %reduce-scatter.47.cloned.1.call-update) | async-done | bytes 208
  1148.6 73.2 %reduce-scatter.49.cloned.1.call-done = f32[16,3]{1,0:T(8,128)} async-done(((f32[256,3]{1,0:T(8,128)}), f32[16,3]{1,0:T(8,128)}) %reduce-scatter.49.cloned.1.call-update) | async-done | bytes 208
  1223.2 72.9 %reduce-scatter.51.cloned.1.call-done = f32[16,3]{1,0:T(8,128)} async-done(((f32[256,3]{1,0:T(8,128)}), f32[16,3]{1,0:T(8,128)}) %reduce-scatter.51.cloned.1.call-update) | async-done | bytes 208
  1297.4 74.4 %reduce-scatter.27.cloned.1.call-done = f32[256,32]{0,1:T(8,128)} async-done(((f32[256,512]{0,1:T(8,128)}), f32[256,32]{0,1:T(8,128)}) %reduce-scatter.27.cloned.1.call-update) | async-done | bytes 32784 | tf_op jit(solution)/shard_map/reduce_scatter | solution.py:341
  1371.9 75.7 %reduce-scatter.29.cloned.1.call-done = f32[256,32]{0,1:T(8,128)} async-done(((f32[256,512]{0,1:T(8,128)}), f32[256,32]{0,1:T(8,128)}) %reduce-scatter.29.cloned.1.call-update) | async-done | bytes 32784 | tf_op jit(solution)/shard_map/reduce_scatter | solution.py:342
  1447.6 75.7 %reduce-scatter.31.cloned.1.call-done = f32[256,32]{0,1:T(8,128)} async-done(((f32[256,512]{0,1:T(8,128)}), f32[256,32]{0,1:T(8,128)}) %reduce-scatter.31.cloned.1.call-update) | async-done | bytes 32784 | tf_op jit(solution)/shard_map/reduce_scatter | solution.py:343
  1523.3 75.6 %reduce-scatter.37.cloned.1.call-done = f32[256,32]{0,1:T(8,128)} async-done(((f32[256,512]{0,1:T(8,128)}), f32[256,32]{0,1:T(8,128)}) %reduce-scatter.37.cloned.1.call-update) | async-done | bytes 32784 | tf_op jit(solution)/shard_map/reduce_scatter | solution.py:346
  1598.9 75.9 %reduce-scatter.39.cloned.1.call-done = f32[256,32]{0,1:T(8,128)} async-done(((f32[256,512]{0,1:T(8,128)}), f32[256,32]{0,1:T(8,128)}) %reduce-scatter.39.cloned.1.call-update) | async-done | bytes 32784 | tf_op jit(solution)/shard_map/reduce_scatter | solution.py:347
  1674.8 75.6 %reduce-scatter.33.cloned.1.call-done = f32[256,32]{0,1:T(8,128)} async-done(((f32[256,512]{0,1:T(8,128)}), f32[256,32]{0,1:T(8,128)}) %reduce-scatter.33.cloned.1.call-update) | async-done | bytes 32784 | tf_op jit(solution)/shard_map/reduce_scatter | solution.py:344
  1750.4 75.9 %reduce-scatter.35.cloned.1.call-done = f32[256,32]{0,1:T(8,128)} async-done(((f32[256,512]{0,1:T(8,128)}), f32[256,32]{0,1:T(8,128)}) %reduce-scatter.35.cloned.1.call-update) | async-done | bytes 32784 | tf_op jit(solution)/shard_map/reduce_scatter | solution.py:345
  1826.3 75.7 %reduce-scatter.41.cloned.1.call-done = f32[256,32]{0,1:T(8,128)} async-done(((f32[256,512]{0,1:T(8,128)}), f32[256,32]{0,1:T(8,128)}) %reduce-scatter.41.cloned.1.call-update) | async-done | bytes 32784 | tf_op jit(solution)/shard_map/reduce_scatter | solution.py:348
  1902.0 79.9 %reduce-scatter.43.cloned.1.call-done = f32[256,128]{1,0:T(8,128)} async-done(((f32[256,2048]{1,0:T(8,128)}), f32[256,128]{1,0:T(8,128)}) %reduce-scatter.43.cloned.1.call-update) | async-done | bytes 131088 | tf_op jit(solution)/shard_map/reduce_scatter | solution.py:349
  1981.9 80.5 %reduce-scatter.45.cloned.1.call-done = f32[1024,32]{0,1:T(8,128)} async-done(((f32[1024,512]{0,1:T(8,128)}), f32[1024,32]{0,1:T(8,128)}) %reduce-scatter.45.cloned.1.call-update) | async-done | bytes 131088 | tf_op jit(solution)/shard_map/reduce_scatter | solution.py:350
  (870 shorter events, 855.1 us)
Async XLA Ops:
  7.2 316.4 %all-gather.24.cloned.1.call-start = ((), (), s32[]{:S(2)}) async-start(), calls=%async_computation.21 | async-start | bytes 1114112 | tf_op jit(solution)/shard_map/all_gather | solution.py:171
  8.0 318.0 %all-gather.22.cloned.1.call-start = ((), (), s32[]{:S(2)}) async-start(), calls=%async_computation.20 | async-start | bytes 1114112 | tf_op jit(solution)/shard_map/all_gather | solution.py:170
  330.8 48.2 %reduce-scatter.55.cloned.1.call-start = ((), (), s32[]{:S(2)}) async-start(), calls=%async_computation.36 | async-start | bytes 3145728 | tf_op jit(solution)/shard_map/while/body/eval_jaxpr/reduce_scatter | solution.py:15
  548.1 56.8 %all-gather.32.cloned.1.call-start = ((), (), s32[]{:S(2)}) async-start(), calls=%async_computation.45 | async-start | bytes 1572864 | tf_op jit(solution)/shard_map/while/body/eval_jaxpr/all_gather | solution.py:19
  615.2 61.7 %all-gather.38.cloned.1.call-start = ((), (), s32[]{:S(2)}) async-start(), calls=%async_computation.48 | async-start | bytes 3145728 | tf_op jit(solution)/shard_map/while/body/eval_jaxpr/all_gather | solution.py:19
  619.3 65.5 %all-gather.36.cloned.1.call-start = ((), (), s32[]{:S(2)}) async-start(), calls=%async_computation.47 | async-start | bytes 4718592 | tf_op jit(solution)/shard_map/while/body/eval_jaxpr/all_gather | solution.py:19
  697.6 51.6 %reduce-scatter.55.cloned.1.call-start = ((), (), s32[]{:S(2)}) async-start(), calls=%async_computation.36 | async-start | bytes 3145728 | tf_op jit(solution)/shard_map/while/body/eval_jaxpr/reduce_scatter | solution.py:15
  759.2 47.7 %reduce-scatter.61.cloned.1.call-start = ((), (), s32[]{:S(2)}) async-start(), calls=%async_computation.39 | async-start | bytes 3145728 | tf_op jit(solution)/shard_map/while/body/eval_jaxpr/reduce_scatter | solution.py:15
  918.5 56.8 %all-gather.32.cloned.1.call-start = ((), (), s32[]{:S(2)}) async-start(), calls=%async_computation.45 | async-start | bytes 1572864 | tf_op jit(solution)/shard_map/while/body/eval_jaxpr/all_gather | solution.py:19
  985.6 62.6 %all-gather.38.cloned.1.call-start = ((), (), s32[]{:S(2)}) async-start(), calls=%async_computation.48 | async-start | bytes 3145728 | tf_op jit(solution)/shard_map/while/body/eval_jaxpr/all_gather | solution.py:19
  989.7 67.4 %all-gather.36.cloned.1.call-start = ((), (), s32[]{:S(2)}) async-start(), calls=%async_computation.47 | async-start | bytes 4718592 | tf_op jit(solution)/shard_map/while/body/eval_jaxpr/all_gather | solution.py:19
  1067.2 80.1 %reduce-scatter.47.cloned.1.call-start = ((), (), s32[]{:S(2)}) async-start(), calls=%async_computation.32 | async-start | bytes 139264
  1068.8 153.0 %reduce-scatter.49.cloned.1.call-start = ((), (), s32[]{:S(2)}) async-start(), calls=%async_computation.33 | async-start | bytes 139264
  1070.3 225.7 %reduce-scatter.51.cloned.1.call-start = ((), (), s32[]{:S(2)}) async-start(), calls=%async_computation.34 | async-start | bytes 139264
  1071.9 300.0 %reduce-scatter.27.cloned.1.call-start = ((), (), s32[]{:S(2)}) async-start(), calls=%async_computation.22 | async-start | bytes 557056 | tf_op jit(solution)/shard_map/reduce_scatter | solution.py:341
  1072.6 374.9 %reduce-scatter.29.cloned.1.call-start = ((), (), s32[]{:S(2)}) async-start(), calls=%async_computation.23 | async-start | bytes 557056 | tf_op jit(solution)/shard_map/reduce_scatter | solution.py:342
  1073.4 449.9 %reduce-scatter.31.cloned.1.call-start = ((), (), s32[]{:S(2)}) async-start(), calls=%async_computation.24 | async-start | bytes 557056 | tf_op jit(solution)/shard_map/reduce_scatter | solution.py:343
  1074.0 524.9 %reduce-scatter.37.cloned.1.call-start = ((), (), s32[]{:S(2)}) async-start(), calls=%async_computation.27 | async-start | bytes 557056 | tf_op jit(solution)/shard_map/reduce_scatter | solution.py:346
  1074.6 600.2 %reduce-scatter.39.cloned.1.call-start = ((), (), s32[]{:S(2)}) async-start(), calls=%async_computation.28 | async-start | bytes 557056 | tf_op jit(solution)/shard_map/reduce_scatter | solution.py:347
  1075.3 675.1 %reduce-scatter.33.cloned.1.call-start = ((), (), s32[]{:S(2)}) async-start(), calls=%async_computation.25 | async-start | bytes 557056 | tf_op jit(solution)/shard_map/reduce_scatter | solution.py:344
  1077.5 748.8 %reduce-scatter.35.cloned.1.call-start = ((), (), s32[]{:S(2)}) async-start(), calls=%async_computation.26 | async-start | bytes 557056 | tf_op jit(solution)/shard_map/reduce_scatter | solution.py:345
  1079.6 822.4 %reduce-scatter.41.cloned.1.call-start = ((), (), s32[]{:S(2)}) async-start(), calls=%async_computation.29 | async-start | bytes 557056 | tf_op jit(solution)/shard_map/reduce_scatter | solution.py:348
  1080.7 901.3 %reduce-scatter.43.cloned.1.call-start = ((), (), s32[]{:S(2)}) async-start(), calls=%async_computation.30 | async-start | bytes 2228224 | tf_op jit(solution)/shard_map/reduce_scatter | solution.py:349
  1081.4 981.0 %reduce-scatter.45.cloned.1.call-start = ((), (), s32[]{:S(2)}) async-start(), calls=%async_computation.31 | async-start | bytes 2228224 | tf_op jit(solution)/shard_map/reduce_scatter | solution.py:350
  (206 other events, 3064.2 us)
Sparse Core Ops, SparseCore 0:
  10.8 58.1 all-gather.23
  71.8 52.7 all-gather.21
  381.2 13.1 reduce-scatter.58
  452.7 18.0 reduce-scatter.62
  522.0 14.8 all-gather.27
  665.4 13.3 all-gather.35
  697.7 15.6 reduce-scatter.52
  751.6 13.1 reduce-scatter.58
  823.1 17.9 reduce-scatter.62
  892.4 14.8 all-gather.27
  1035.8 13.2 all-gather.35
  1070.3 76.9 reduce-scatter.46
  1149.6 72.1 reduce-scatter.48
  1223.9 72.1 reduce-scatter.50
  1299.0 72.8 reduce-scatter.26
  1374.7 72.8 reduce-scatter.28
  1450.3 72.9 reduce-scatter.30
  1526.0 72.9 reduce-scatter.36
  1601.8 72.9 reduce-scatter.38
  1677.4 72.9 reduce-scatter.32
  1753.3 72.9 reduce-scatter.34
  1829.1 72.8 reduce-scatter.40
  1905.0 76.9 reduce-scatter.42
  1984.7 77.6 reduce-scatter.44
  (19 shorter events, 202.8 us)
where the time goes:
time: 2080 us; the launch traced here: 2070 us
  waiting for transfers between devices  1230 us (59%)
  blocking collectives  355 us (17%)
  matrix products  243 us (12%)
  other arithmetic  114 us (5%)
  local copies, waits for them, and re-layouts  77.7 us (4%)
  loops' own time  33.1 us (2%)
    unnamed x18, waiting for transfers between devices  215 us
    reduce_scatter x14, waiting for transfers between devices, row_total(): lax.psum_scatter(partial_value, 'row', scatter_dimension=2, tiled=True)  145 us
    all_gather x14, waiting for transfers between devices, widen(): return lax.all_gather(gradient, 'row', axis=2, tiled=True)  103 us
    reduce_scatter x1, waiting for transfers between devices, body(): lax.psum_scatter(totals[9], 'col', scatter_dimension=1, tiled=True)  80.5 us
    reduce_scatter x1, waiting for transfers between devices, body(): lax.psum_scatter(totals[8], 'col', scatter_dimension=1, tiled=True)  79.9 us
    reduce_scatter x1, waiting for transfers between devices, body(): lax.psum_scatter(totals[4], 'col', scatter_dimension=1, tiled=True)  75.9 us
    reduce_scatter x1, waiting for transfers between devices, body(): lax.psum_scatter(totals[6], 'col', scatter_dimension=1, tiled=True)  75.9 us
    reduce_scatter x1, waiting for transfers between devices, body(): lax.psum_scatter(totals[7], 'col', scatter_dimension=1, tiled=True)  75.7 us
  transfers between devices with their start and end apart: 43, of which 37 were waited for; matrix products, arithmetic and copies ran while one was open for 8% of the time, Pallas kernels for 0%

commit v1 on v0

v1 whole, which is shorter than its diff:
```python
import jax
import jax.numpy as jnp
from jax import lax
from jax.experimental import pallas as pl
from jax.experimental.pallas import tpu as pltpu
from jax.sharding import PartitionSpec as P

F32 = jnp.float32
BF16 = jnp.bfloat16
EPSILON = 1e-05
MASKED = -1e30
T = 1024
D = 512
H = 8
HD = 64
TB = 256


def dot(left, right, left_dim, right_dim):
    return lax.dot_general(
        left, right, (((left_dim,), (right_dim,)), ((), ())), preferred_element_type=F32
    )


def gelu_both(v):
    root = 0.7978845608028654
    square = v * v
    t = jnp.tanh(root * v * (1.0 + 0.044715 * square))
    half = 0.5 * (1.0 + t)
    slope = half + (0.5 * root) * v * (1.0 - t * t) * (1.0 + (3.0 * 0.044715) * square)
    return v * half, slope


def compute(
    x_hbm, mem_hbm, cot_hbm, w_hbm, par, seg, pad,
    lo_hbm, tg_hbm, mg_hbm, g_hbm, e_hbm,
    xs, cs, xt, mt, w8, wup, wdn, qkv, pay, ctx, cctx, inv, xh0, xh1, rstd,
    flow, slow, tlow, ring, es, sg, gs, pcol, cols, gcol, acc, gsta, gstb,
    sem, esem, asem, bsem,
):
    def weight(r, m):
        return w8[r, :, m * 32:(m + 1) * 32, :].reshape(D, 256)

    def forward(m, source):
        return dot(weight(0, m), source[0:256], 1, 0) + dot(weight(1, m), source[256:512], 1, 0)

    def param(k):
        return pcol[:, k:k + 1]

    def add_col(k, value):
        cols[k] = cols[k] + (value[:, 0:128] + value[:, 128:256])

    loads = [
        pltpu.make_async_copy(x_hbm, xs.at[0], sem.at[0]),
        pltpu.make_async_copy(mem_hbm, xs.at[1], sem.at[1]),
        pltpu.make_async_copy(cot_hbm, cs, sem.at[2]),
        pltpu.make_async_copy(w_hbm.at[:, :, pl.ds(0, 256), :], w8, sem.at[3]),
        pltpu.make_async_copy(w_hbm.at[:, :, pl.ds(256, 128), :], wup, sem.at[4]),
        pltpu.make_async_copy(w_hbm.at[:, :, pl.ds(384, 128), :], wdn, sem.at[5]),
    ]
    for copy in loads:
        copy.start()
    pcol[...] = jnp.concatenate([par[...].T, jnp.zeros((D, 112), F32)], axis=1)
    cols[...] = jnp.zeros_like(cols)

    padlen = jnp.sum(pad[...], axis=1, keepdims=True)

    @pl.loop(0, 4)
    def _(j):
        at = pl.multiple_of(j * 256, 256)
        low = seg[:, pl.ds(at, 256)]
        here = at + lax.broadcasted_iota(jnp.int32, (1, 256), 1)
        high = jnp.minimum(here, padlen - 1)
        rows = lax.broadcasted_iota(jnp.int32, (T, 256), 0)
        fits = ((rows >= low) & (rows <= high)) | (rows == here)
        ring[0, :, pl.ds(at, 256)] = jnp.where(fits, 0.0, MASKED).astype(BF16)

    loads[0].wait()
    for r in range(2):
        xt[256 * r:256 * r + 256] = xs[0, r].T
    loads[1].wait()
    for r in range(2):
        mt[256 * r:256 * r + 256] = xs[1, r].T
    loads[3].wait()

    for m in range(3):
        out = forward(m, xt)
        if m == 0:
            out = out * 0.125
        qkv[m] = out.astype(BF16).reshape(H, HD, T)
    for m in (5, 6):
        pay[m - 4] = forward(m, mt).astype(BF16).reshape(H, HD, T)

    ones = jnp.ones((16, T), BF16)

    def attend(q, k, v, q_at, width, keys, masked):
        s = dot(k[:, 0:keys], q[:, q_at:q_at + width], 0, 0)
        if masked:
            s = s + ring[0, 0:keys, q_at:q_at + width].astype(F32)
        top = jnp.max(s, axis=0, keepdims=True)
        e = jnp.exp(s - top).astype(BF16)
        both = dot(v[:, 0:keys], e, 1, 0)
        inverse = 1.0 / both[HD:HD + 1]
        return e, both[0:HD] * inverse, inverse

    def self_tile(i, j):
        if j == 3:
            return 0, 256 * i
        if j == 1:
            return 512 * i, 1024
        return (0 if j == 0 else 256), 512 + 256 * i

    @pl.loop(0, 4)
    def _(pair):
        for i in range(2):
            h = pair * 2 + i
            v = jnp.concatenate([qkv[2, h], ones], axis=0)
            for j in range(4):
                keys = 256 * (j + 1)
                at = slice(256 * j, 256 * j + 256)
                e, out, inverse = attend(qkv[0, h], qkv[1, h], v, 256 * j, 256, keys, True)
                row, lane = self_tile(i, j)
                es[pair, row:row + keys, lane:lane + 256] = e
                ctx[h, :, at] = out.astype(BF16)
                inv[0, h, :, at] = inverse

    def norm(total):
        average = jnp.mean(total, axis=0, keepdims=True)
        centred = total - average
        factor = lax.rsqrt(jnp.mean(centred * centred, axis=0, keepdims=True) + EPSILON)
        return centred * factor, factor

    @pl.loop(0, 4)
    def _(tb):
        at = pl.ds(pl.multiple_of(tb * TB, TB), TB)
        out = forward(3, ctx[:, :, at].reshape(D, TB))
        normed, factor = norm(param(6) * xt[:, at].astype(F32) + out)
        xh0[:, at] = normed
        rstd[0, :, at] = factor
        flow[:, at] = (normed * param(0) + param(3)).astype(BF16)

    pay[0] = (forward(4, flow) * 0.125).astype(BF16).reshape(H, HD, T)

    def e_out(h, slot):
        return pltpu.make_async_copy(ring.at[slot], e_hbm.at[h], esem.at[slot])

    def e_in(h, slot):
        return pltpu.make_async_copy(e_hbm.at[h], ring.at[slot], esem.at[slot])

    @pl.loop(0, 2)
    def _(four):
        for slot in range(4):
            h = four * 4 + slot

            @pl.when(four > 0)
            def _():
                e_out(slot, slot).wait()

            v = jnp.concatenate([pay[2, h], ones], axis=0)
            for j in range(2):
                at = slice(512 * j, 512 * j + 512)
                e, out, inverse = attend(pay[0, h], pay[1, h], v, 512 * j, 512, T, False)
                ring[slot, :, at] = e
                cctx[h, :, at] = out.astype(BF16)
                inv[1, h, :, at] = inverse
            e_out(h, slot).start()

    @pl.loop(0, 4)
    def _(tb):
        at = pl.ds(pl.multiple_of(tb * TB, TB), TB)
        out = forward(7, cctx[:, :, at].reshape(D, TB))
        first = xh0[:, at] * param(0) + param(3)
        normed, factor = norm(param(7) * first + out)
        xh1[:, at] = normed
        rstd[1, :, at] = factor
        slow[:, at] = (normed * param(1) + param(4)).astype(BF16)

    for slot in range(4):
        e_out(4 + slot, slot).wait()
    loads[4].wait()
    loads[5].wait()
    loads[2].wait()

    def up(r, b):
        return wup[r, 4 * b:4 * b + 4].reshape(512, 256)

    def down(b):
        return wdn[b // 4, :, 32 * (b % 4):32 * (b % 4) + 32, :].reshape(D, 256)

    for b in range(4):
        place = slice(512 * (b % 2), 512 * (b % 2) + 512)
        for t in range(2):
            at = slice(512 * t, 512 * t + 512)
            v = dot(up(0, b), slow[0:256, at], 1, 0) + dot(up(1, b), slow[256:512, at], 1, 0)
            value, slope = gelu_both(v)
            ring[b // 2, place, at] = value.astype(BF16)
            ring[2 + b // 2, place, at] = slope.astype(BF16)

    def norm_back(upstream, normed, factor, k):
        scaled = upstream * param(k)
        one = jnp.mean(scaled, axis=0, keepdims=True)
        two = jnp.mean(scaled * normed, axis=0, keepdims=True)
        add_col(k, upstream * normed)
        add_col(3 + k, upstream)
        return factor * (scaled - one - normed * two)

    @pl.loop(0, 4)
    def _(tb):
        at = pl.ds(pl.multiple_of(tb * TB, TB), TB)
        out = None
        for b in range(8):
            part = dot(down(b), ring[b // 4, 256 * (b % 4):256 * (b % 4) + 256, at], 1, 0)
            out = part if out is None else out + part
        second = xh1[:, at] * param(1) + param(4)
        normed, factor = norm(param(8) * second + out)
        final = (normed * param(2) + param(5)).astype(BF16)
        upstream = jnp.concatenate([cs[0, at, :].T, cs[1, at, :].T], axis=0).astype(F32)
        for r in range(2):
            xs[0, r, at, :] = final[256 * r:256 * r + 256].T
        third = norm_back(upstream, normed, factor, 2)
        add_col(8, third * second)
        sg[:, at] = param(8) * third
        tlow[:, at] = third.astype(BF16)

    lo_out = pltpu.make_async_copy(xs.at[0], lo_hbm, sem.at[0])
    lo_out.start()

    pending = {}

    def send(key, source, target, which):
        pending[key] = pltpu.make_async_copy(source, target, which)
        pending[key].start()

    def settle(key):
        if key in pending:
            pending.pop(key).wait()

    turn = [0]

    def rows_out(r, row, value):
        slot = turn[0] % 4
        turn[0] += 1
        settle(("a", slot))
        gsta[slot] = value.astype(BF16).reshape(16, 32, 256)
        send(("a", slot), gsta.at[slot], g_hbm.at[r, :, pl.ds(row, 32), :], asem.at[slot])

    def square_grad(m, left, right):
        for r in range(2):
            rows_out(r, 32 * m, dot(left, right[256 * r:256 * r + 256], 1, 1))

    for f in range(8):
        rows = slice(256 * (f % 4), 256 * (f % 4) + 256)
        rows_out(f // 4, 384 + 32 * (f % 4), dot(tlow[...], ring[f // 4, rows, :], 1, 1))
        grad = dot(down(f), tlow[...], 0, 0) * ring[2 + f // 4, rows, :].astype(F32)
        ring[2 + f // 4, rows, :] = grad.astype(BF16)
    for b in range(4):
        grad = ring[2 + b // 2, 512 * (b % 2):512 * (b % 2) + 512, :]
        for r in range(2):
            settle(("b", r))
            part = dot(grad, slow[256 * r:256 * r + 256], 1, 1)
            gstb[r] = part.astype(BF16).reshape(4, 128, 256)
            send(
                ("b", r), gstb.at[r], g_hbm.at[r, pl.ds(4 * b, 4), pl.ds(256, 128), :], bsem.at[r]
            )
    for r in range(2):
        half = slice(256 * r, 256 * r + 256)
        for t in range(2):
            at = slice(512 * t, 512 * t + 512)
            part = None
            for b in range(4):
                place = slice(512 * (b % 2), 512 * (b % 2) + 512)
                one = dot(up(r, b), ring[2 + b // 2, place, at], 0, 0)
                part = one if part is None else part + one
            sg[half, at] = sg[half, at] + part

    for slot in range(4):
        e_in(slot, slot).start()

    @pl.loop(0, 4)
    def _(tb):
        at = pl.ds(pl.multiple_of(tb * TB, TB), TB)
        middle = norm_back(sg[:, at], xh1[:, at], rstd[1, :, at], 1)
        add_col(7, middle * (xh0[:, at] * param(0) + param(3)))
        sg[:, at] = param(7) * middle
        tlow[:, at] = middle.astype(BF16)

    square_grad(7, tlow[...], cctx[...].reshape(D, T))
    for r in range(2):
        slow[256 * r:256 * r + 256] = dot(weight(r, 7), tlow[...], 0, 0).astype(BF16)

    def scaled_grad(context, which, h):
        rows = pl.ds(pl.multiple_of(h * HD, HD), HD)
        g = (slow[rows, :].astype(F32) * inv[which, h]).astype(BF16)
        delta = jnp.sum(g.astype(F32) * context[h].astype(F32), axis=0, keepdims=True)
        return g, delta

    @pl.loop(0, 2)
    def _(four):
        for slot in range(4):
            h = four * 4 + slot
            e_in(h, slot).wait()
            g, delta = scaled_grad(cctx, 1, h)
            q, k, v = pay[0, h], pay[1, h], pay[2, h]
            dp = dot(v, g, 0, 0)
            e = ring[slot]
            ds = e * (dp - delta).astype(BF16)
            pay[0, h] = (dot(k, ds, 1, 0) * 0.125).astype(BF16)
            pay[1, h] = dot(q, ds, 1, 1).astype(BF16)
            pay[2, h] = dot(g, e, 1, 1).astype(BF16)

            @pl.when(four == 0)
            def _():
                e_in(h + 4, slot).start()

    grads = [pay[i].reshape(D, T) for i in range(3)]
    square_grad(4, grads[0], flow)
    square_grad(5, grads[1], mt)
    square_grad(6, grads[2], mt)
    for r in range(2):
        out = dot(weight(r, 5), grads[1], 0, 0) + dot(weight(r, 6), grads[2], 0, 0)
        gs[r] = out.T
    mg_out = pltpu.make_async_copy(gs, mg_hbm, sem.at[1])
    mg_out.start()
    for r in range(2):
        half = slice(256 * r, 256 * r + 256)
        sg[half] = sg[half] + dot(weight(r, 4), grads[0], 0, 0)

    @pl.loop(0, 4)
    def _(tb):
        at = pl.ds(pl.multiple_of(tb * TB, TB), TB)
        inner = norm_back(sg[:, at], xh0[:, at], rstd[0, :, at], 0)
        add_col(6, inner * xt[:, at].astype(F32))
        sg[:, at] = param(6) * inner
        tlow[:, at] = inner.astype(BF16)

    for k in range(9):
        gcol[:, k:k + 1] = jnp.sum(cols[k], axis=1, keepdims=True)

    square_grad(3, tlow[...], ctx[...].reshape(D, T))
    for r in range(2):
        slow[256 * r:256 * r + 256] = dot(weight(r, 3), tlow[...], 0, 0).astype(BF16)

    @pl.loop(0, 4)
    def _(pair):
        for i in range(2):
            h = pair * 2 + i
            g, delta = scaled_grad(ctx, 0, h)
            q, k, v = qkv[0, h], qkv[1, h], qkv[2, h]
            for j in (3, 2, 1, 0):
                keys = 256 * (j + 1)
                at = slice(256 * j, 256 * j + 256)
                row, lane = self_tile(i, j)
                e = es[pair, row:row + keys, lane:lane + 256]
                dp = dot(v[:, 0:keys], g[:, at], 0, 0)
                ds = e * (dp - delta[:, at]).astype(BF16)
                qkv[0, h, :, at] = (dot(k[:, 0:keys], ds, 1, 0) * 0.125).astype(BF16)
                new_k = dot(q[:, at], ds, 1, 1)
                new_v = dot(g[:, at], e, 1, 1)
                if j == 3:
                    acc[i, 0] = new_k
                    acc[i, 1] = new_v
                else:
                    acc[i, 0, :, 0:keys] = acc[i, 0, :, 0:keys] + new_k
                    acc[i, 1, :, 0:keys] = acc[i, 1, :, 0:keys] + new_v
            qkv[1, h] = acc[i, 0].astype(BF16)
            qkv[2, h] = acc[i, 1].astype(BF16)

    grads = [qkv[i].reshape(D, T) for i in range(3)]
    for m in range(3):
        square_grad(m, grads[m], xt)
    mg_out.wait()
    for r in range(2):
        out = sg[256 * r:256 * r + 256]
        for m in range(3):
            out = out + dot(weight(r, m), grads[m], 0, 0)
        gs[r] = out.T
    tg_out = pltpu.make_async_copy(gs, tg_hbm, sem.at[1])
    tg_out.start()
    tg_out.wait()
    lo_out.wait()
    for key in list(pending):
        settle(key)


def run_compute(x, mem, cot, w, par, seg, pad):
    anywhere = pl.BlockSpec(memory_space=pl.ANY)
    vmem = pl.BlockSpec(memory_space=pltpu.VMEM)
    V = pltpu.VMEM
    scratch = [
        V((2, 2, T, 256), BF16), V((2, T, 256), BF16),
        V((D, T), BF16), V((D, T), BF16),
        V((2, 16, 256, 256), BF16), V((2, 16, 128, 256), BF16), V((2, 16, 128, 256), BF16),
        V((3, H, HD, T), BF16), V((3, H, HD, T), BF16),
        V((H, HD, T), BF16), V((H, HD, T), BF16),
        V((2, H, 1, T), F32),
        V((D, T), F32), V((D, T), F32), V((2, 1, T), F32),
        V((D, T), BF16), V((D, T), BF16), V((D, T), BF16),
        V((4, T, T), BF16), V((4, T, 1280), BF16),
        V((D, T), F32), V((2, T, 256), F32),
        V((D, 128), F32), V((9, D, 128), F32),
        V((2, 2, HD, T), F32),
        V((4, 16, 32, 256), BF16), V((2, 4, 128, 256), BF16),
        pltpu.SemaphoreType.DMA((6,)), pltpu.SemaphoreType.DMA((4,)),
        pltpu.SemaphoreType.DMA((4,)), pltpu.SemaphoreType.DMA((2,)),
    ]
    shape = jax.ShapeDtypeStruct
    return pl.pallas_call(
        lambda *refs: compute(*refs[:12], *refs[13:37], refs[12], *refs[37:]),
        in_specs=[anywhere] * 4 + [vmem] * 3,
        out_specs=[anywhere] * 5 + [vmem],
        out_shape=[
            shape((2, T, 256), BF16), shape((2, T, 256), F32), shape((2, T, 256), F32),
            shape((2, 16, 512, 256), BF16), shape((H, T, T), BF16), shape((D, 128), F32),
        ],
        scratch_shapes=scratch,
        compiler_params=pltpu.CompilerParams(vmem_limit_bytes=63 * 2**20),
        name="layer",
    )(x, mem, cot, w, par, seg, pad)


CHIPS = 16


def to_sixteen(w):
    n = w.shape[1]
    if n == CHIPS:
        return w
    part = D // n

    def spread(block):
        block = block.reshape(2, n, -1, part, 256).swapaxes(1, 2).reshape(2, -1, CHIPS, 32, 256)
        return block.swapaxes(1, 2).reshape(2, CHIPS, -1, 256)

    return jnp.concatenate(
        [
            spread(w[:, :, :8 * part]),
            w[:, :, 8 * part:12 * part].reshape(2, CHIPS, 128, 256),
            spread(w[:, :, 12 * part:]),
        ],
        axis=2,
    )


def from_sixteen(g, n):
    if n == CHIPS:
        return g
    part = D // n

    def gather(block):
        block = block.reshape(2, CHIPS, -1, 32, 256).swapaxes(1, 2).reshape(2, -1, n, part, 256)
        return block.swapaxes(1, 2).reshape(2, n, -1, 256)

    return jnp.concatenate(
        [
            gather(g[:, :, :256]),
            g[:, :, 256:384].reshape(2, n, 4 * part, 256),
            gather(g[:, :, 384:]),
        ],
        axis=2,
    )


def body(
    tokens, memory, cotangent, segments, padding,
    self_query, self_key, self_value, self_output,
    cross_query, cross_key, cross_value, cross_output,
    feed_up, feed_down, norm_gain, norm_bias, omegas,
):
    row = lax.axis_index("row")
    n = lax.axis_size("col")
    part = D // n
    squares = (
        self_query, self_key, self_value, self_output,
        cross_query, cross_key, cross_value, cross_output,
    )
    blob = jnp.concatenate(
        [m.T for m in squares]
        + [feed_up.T]
        + [feed_down.T[:, 256 * s:256 * s + 256] for s in range(4)],
        axis=0,
    )
    w = lax.all_gather(blob, ("row", "col"), axis=0, tiled=False).reshape(2, n, 16 * part, 256)
    w = to_sixteen(w)
    par = jnp.concatenate([norm_gain, norm_bias, omegas], axis=0)
    par = lax.all_gather(par, "row", axis=1, tiled=True)
    par = jnp.concatenate([par, jnp.zeros((7, D), F32)], axis=0)

    def mine(array):
        return lax.all_to_all(array, "row", split_axis=0, concat_axis=0, tiled=True)

    seg = lax.dynamic_slice_in_dim(segments, row, 1, 0)
    pad = lax.dynamic_slice_in_dim(padding, row, 1, 0)
    lo, tg, mg, g, _, gcol = run_compute(mine(tokens), mine(memory), mine(cotangent), w, par, seg, pad)
    lo, tg, mg = mine(lo), mine(tg), mine(mg)
    g = from_sixteen(g, n).reshape(2 * n, 16 * part, 256)
    g = lax.psum_scatter(g, ("row", "col"), scatter_dimension=0, tiled=False)
    gcol = lax.psum_scatter(
        gcol.reshape(2 * n, part // 2, 128), ("row", "col"), scatter_dimension=0, tiled=False
    )
    g = g.astype(F32)
    small = gcol[:, 0:9].T
    last = 12 * part
    return (
        lo, tg, mg,
        *[g[part * m:part * m + part].T for m in range(8)],
        g[8 * part:last].T,
        jnp.concatenate([g[last + part * s:last + part * s + part].T for s in range(4)], axis=0),
        small[0:3], small[3:6], small[6:9],
    )


def solution(mesh):
    wide = P(None, "col", "row")
    square = P("row", "col")
    return jax.shard_map(
        body,
        mesh=mesh,
        in_specs=(wide,) * 3 + (P(None, "col"),) * 2 + (square,) * 10 + (P(None, "row"),) * 3,
        out_specs=(wide,) * 3 + (square,) * 10 + (P(None, ("row", "col")),) * 3,
        check_vma=False,
    )
```

time: 2080 us -> 603 us (0.29)
  waiting for transfers between devices: 1230 us -> 386 us
  blocking collectives: 355 us -> 29.3 us
  matrix products: 243 us -> 0 us
  Pallas kernels: 0 us -> 126 us
  other arithmetic: 114 us -> 1.66 us
  local copies, waits for them, and re-layouts: 77.7 us -> 33.2 us
  loops' own time: 33.1 us -> 0 us
    reduce_scatter x24 -> x2, waiting for transfers between devices: 910 us -> 305 us  [the longest x1 182 us: body(): g = lax.psum_scatter(g, ('row', 'col'), scatter_dimension=0, tiled=False)]
    all_gather x8 -> x1, blocking collectives: 311 us -> 1.94 us  [body(): par = lax.all_gather(par, 'row', axis=1, tiled=True)]
    dot_general x98 -> x0, matrix products: 243 us -> none  [the longest x14 50.3 us: row_total(): jnp.einsum('nd,sdo->sno', acts_in, matrices, preferred_element_type=jnp.f...]
    unnamed x18 -> x3, waiting for transfers between devices: 215 us -> 0.7 us
    pallas_call x0 -> x1, Pallas kernels: none -> 126 us  [run_compute(): pl.pallas_call(lambda *refs: compute(*refs[:12], *refs[13:37], refs[12],...]
    reduce_sum x26 -> x0, other arithmetic: 51.4 us -> none  [the longest x8 16.3 us: one_block(): totals = jnp.sum(raised, axis=2, keepdims=True)]
    psum x18 -> x0, blocking collectives: 44.7 us -> none  [the longest x6 15 us: layer_norm(): average = lax.psum(jnp.sum(resid, axis=1), 'row') / features]
    convert_element_type x18 -> x1, other arithmetic: 35 us -> 0.98 us  [body(): g = g.astype(F32)]
  transfers between devices with their start and end apart: 43 -> 4, of which waited for: 37 -> 3; matrix products, arithmetic and copies ran while one was open for 8% -> 2% of each run, Pallas kernels for 0% -> 0%
where the time goes in v1:
time: 603 us; the launch traced here: 595 us
  waiting for transfers between devices  386 us (64%)
  Pallas kernels  126 us (21%)
  local copies, waits for them, and re-layouts  33.2 us (6%)
  blocking collectives  29.3 us (5%)
  between operations  14.4 us (2%)
    reduce_scatter x1, waiting for transfers between devices, body(): g = lax.psum_scatter(g, ('row', 'col'), scatter_dimension=0, tiled=False)  182 us
    pallas_call x1, Pallas kernels, run_compute(): pl.pallas_call(lambda *refs: compute(*refs[:12], *refs[13:37], refs[12],...  126 us
    reduce_scatter x1, waiting for transfers between devices, body(): lax.psum_scatter(gcol.reshape(2 * n, part // 2, 128), ('row', 'col'), sca...  123 us
    all_gather x1, waiting for transfers between devices, body(): lax.all_gather(blob, ('row', 'col'), axis=0, tiled=False)  80.5 us
    all_to_all x5, blocking collectives, mine(): return lax.all_to_all(array, 'row', split_axis=0, concat_axis=0, tiled=True)  27.4 us
    unnamed x36, local copies, waits for them, and re-layouts  12.7 us
  transfers between devices with their start and end apart: 4, of which 3 were waited for; matrix products, arithmetic and copies ran while one was open for 2% of the time, Pallas kernels for 0%

profile of v1, /device:TPU:0, one launch (start us, length us, event | category | flops | bytes accessed | tf_op | source)
XLA Modules:
  0.0 594.7 jit_solution(8290553422350795956)
XLA Ops:
  8.1 0.8 copy.35
  8.9 0.8 copy.36
  9.7 0.8 copy.37
  11.5 0.9 copy.39
  13.2 0.8 copy.41
  15.3 1.8 concatenate.12
  17.1 3.6 all-to-all-start
  20.8 1.9 all_gather.11
  24.0 80.5 %all-gather.3.cloned.1.call-done = bf16[16384,256]{0,1:T(8,128)(2,1)} async-done(((bf16[512,256]{0,1:T(8,128)(2,1)}), bf16[16384,256]{0,1:T(8,128)(2,1)}) %all-gather.3.cloned.1.call-update) | async-done | bytes 8388624 | tf_op jit(solution)/shard_map/all_gather | solution.py:482
  104.5 11.4 %copy.46 = bf16[16384,256]{1,0:T(8,128)(2,1)} copy(bf16[16384,256]{0,1:T(8,128)(2,1)} %all-gather.3.cloned.1.call-done) | data formatting | bytes 16777216 | tf_op jit(solution)/shard_map/all_gather | solution.py:482
  115.9 5.5 all_to_all.30.refs_1_
  121.4 5.4 all_to_all.31.refs_2_
  126.8 126.3 %layer.1 = (bf16[2,1024,256]{2,1,0:T(8,128)(2,1)}, f32[2,1024,256]{2,1,0:T(8,128)}, f32[2,1024,256]{2,1,0:T(8,128)}, bf16[2,16,512,256]{3,2,1,0:T(8,128)(2,1)}, ...) custom-call(bf16[2,1024,256]{2,1,0:T(8,128)(2,1)} %copy-done.1, bf16[2,1024,256]{2,1,0:T(8,128)(2,1)} %all_to_all.30.refs_1_, ...), custom_call_target="tpu_custom_call" | custom-call | tf_op jit(solution)/shard_map/layer/pallas_call | solution.py:407
  253.1 2.9 copy.47
  257.3 4.7 all_to_all.32
  262.0 5.5 all_to_all.33
  267.5 6.3 %all_to_all.34 = f32[2,1024,256]{2,1,0:T(8,128)} all-to-all(f32[2,1024,256]{2,1,0:T(8,128)S(1)} %copy-done.2), channel_id=1, replica_groups=mesh['row'=2,'col'=16] {'row'}, dimensions={0} | all-to-all | bytes 4194304 | tf_op jit(solution)/shard_map/all_to_all | solution.py:489
  273.8 122.8 %reduce-scatter.5.cloned.1.call-done = f32[1,16,128]{1,2,0:T(8,128)} async-done(((f32[32,16,128]{1,2,0:T(8,128)}), f32[1,16,128]{1,2,0:T(8,128)}) %reduce-scatter.5.cloned.1.call-update) | async-done | bytes 8208 | tf_op jit(solution)/shard_map/reduce_scatter | solution.py:497
  398.0 182.0 %reduce-scatter.3.cloned.1.call-done = bf16[1,512,256]{2,1,0:T(8,128)(2,1)} async-done(((bf16[32,512,256]{2,1,0:T(8,128)(2,1)}), bf16[1,512,256]{2,1,0:T(8,128)(2,1)}) %reduce-scatter.3.cloned.1.call-update) | async-done | bytes 262160 | tf_op jit(solution)/shard_map/reduce_scatter | solution.py:496
  580.0 1.0 convert_element_type.4
  583.1 1.0 copy.52
  584.1 1.3 copy.53
  585.4 1.0 copy-done
  586.4 1.3 copy.54
  (47 shorter events, 9.8 us)
Async XLA Ops:
  7.2 97.3 %all-gather.3.cloned.1.call-start = ((), (), s32[]{:S(2)}) async-start(), calls=%async_computation.10 | async-start | bytes 8650752 | tf_op jit(solution)/shard_map/all_gather | solution.py:482
  11.4 9.3 %copy-start.7 = (f32[3,256]{1,0:T(4,128)S(1)}, f32[3,256]{1,0:T(4,128)}, u32[]{:S(2)}) copy-start(f32[3,256]{1,0:T(4,128)} %param.35) | copy-start | bytes 9220
  11.4 9.3 %copy-start.8 = (f32[3,256]{1,0:T(4,128)S(1)}, f32[3,256]{1,0:T(4,128)}, u32[]{:S(2)}) copy-start(f32[3,256]{1,0:T(4,128)} %param.34) | copy-start | bytes 9220
  11.4 9.3 %copy-start.9 = (f32[3,256]{1,0:T(4,128)S(1)}, f32[3,256]{1,0:T(4,128)}, u32[]{:S(2)}) copy-start(f32[3,256]{1,0:T(4,128)} %param.33) | copy-start | bytes 9220
  13.1 10.2 %copy-start.10 = (s32[2,1024]{1,0:T(2,128)S(1)}, s32[2,1024]{1,0:T(2,128)}, u32[]{:S(2)}) copy-start(s32[2,1024]{1,0:T(2,128)} %param.22) | copy-start | bytes 24580
  13.2 10.2 %copy-start.11 = (s32[2,1024]{1,0:T(2,128)S(1)}, s32[2,1024]{1,0:T(2,128)}, u32[]{:S(2)}) copy-start(s32[2,1024]{1,0:T(2,128)} %param.21) | copy-start | bytes 24580
  17.1 98.8 %all-to-all-start = ((bf16[2,1024,256]{2,1,0:T(8,128)(2,1)}), bf16[2,1024,256]{2,1,0:T(8,128)(2,1)S(1)}, u32[]{:S(2)}, u32[]{:S(2)}) async-start(bf16[2,1024,256]{2,1,0:T(8,128)(2,1)} %param.18), calls=%async_computation | async-start | bytes 2097152 | tf_op jit(solution)/shard_map/all_to_all | solution.py:489
  20.7 376.0 %reduce-scatter.5.cloned.1.call-start = ((), (), s32[]{:S(2)}) async-start(), calls=%async_computation.9 | async-start | bytes 2162688 | tf_op jit(solution)/shard_map/reduce_scatter | solution.py:497
  24.0 91.9 %copy-start.4 = (bf16[2,1024,256]{2,1,0:T(8,128)(2,1)S(1)}, bf16[2,1024,256]{2,1,0:T(8,128)(2,1)}, u32[]{:S(2)}) copy-start(bf16[2,1024,256]{2,1,0:T(8,128)(2,1)} %param.19) | copy-start | bytes 3145732
  115.9 5.5 copy-start.5
  115.9 10.9 %copy-start.1 = (bf16[2,1024,256]{2,1,0:T(8,128)(2,1)}, bf16[2,1024,256]{2,1,0:T(8,128)(2,1)S(1)}, u32[]{:S(2)}) copy-start(bf16[2,1024,256]{2,1,0:T(8,128)(2,1)S(1)} %all-to-all-done.refs_0_) | copy-start | bytes 3145732
  256.0 323.9 %reduce-scatter.3.cloned.1.call-start = ((), (), s32[]{:S(2)}) async-start(), calls=%async_computation.8 | async-start | bytes 8650752 | tf_op jit(solution)/shard_map/reduce_scatter | solution.py:496
  256.1 1.2 copy-start.6
  256.8 5.2 copy-start.3
  262.0 5.5 copy-start.2
  584.1 2.3 copy-start
Sparse Core Ops, SparseCore 0:
  17.2 87.2 all-gather.2
  256.1 140.4 reduce-scatter.4
  399.1 180.8 reduce-scatter.2
